TPU v7x, 512 devices: a whole 4x4x16 slice. The times are simulated.
512 devices in a mesh: gz: 64 (over y, z), xy: 8 (over x, core).
Axes of the slice: x: 4, y: 4, z: 16, core: 2. Of those that a mesh axis runs over, the one named last changes fastest.
Arguments:
- right_side: float32 [2, 64, 64, 2048], P(None, 'gz', 'xy')
- stiff_across: float32 [64, 64, 2048], P('gz', 'xy'), may hold values from 0.3 to 3
- stiff_down: float32 [64, 64, 2048], P('gz', 'xy'), may hold values from 0.3 to 3
- anchor: float32 [64, 64, 2048], P('gz', 'xy'), may hold values from 0.02 to 0.2
- source_node: int32 [64, 8, 1024], P('gz', 'xy'), may hold values from 0 to 16383
- target_cell: int32 [64, 8, 1024], P('gz', 'xy'), may hold values from 0 to 14334, as said below
- corner_weight: float32 [4, 64, 8, 1024], P(None, 'gz', 'xy'), may hold values from 0 to 1, as said below
- block_count: int32 [64, 8], P('gz', 'xy'), may hold values from 1 to 8, as said below
Outputs:
- solution_field: float32 [2, 64, 64, 2048], P(None, 'gz', 'xy')
- residual: float32 [2, 64, 64, 2048], P(None, 'gz', 'xy')
Inputs may be any that keep to these rules, and one draw needn't show every extreme that they name: `target_cell`: each target cell's row is below 7 and its column below 2047 within the block, so all four corners lie in the same block. `corner_weight`: the weights of a slot are nonnegative and sum to 1. `block_count`: some device holds exactly 8 used blocks.
All inputs are finite; a program needn't handle non-finite values.
Results may differ from a plain program's by a relative error of at most 0.00013.
Values sent between devices are 32-bit elements; how exact they have to be, the bound alone decides.
A program may use at most 64 MiB of HBM per device.

v0:
```python
import jax
import jax.numpy as jnp
from jax import lax
from jax.sharding import Mesh
from jax.sharding import PartitionSpec as P

BLOCK = 128
ITERS = 3
GZ_XY = ("gz_0", "gz_1", "xy_0", "xy_1")
GZ = ("gz_0", "gz_1")
XY = ("xy_0", "xy_1")


def one_axis_at_a_time(shard, axes):
    for axis in axes:
        shard = lax.psum(shard, axis)
    return shard


def passed_along(block, axis, distance):
    devices = range(lax.axis_size(axis))
    route = [(i - distance, i) for i in devices if i - distance in devices]
    return lax.ppermute(block, axis, route)


def padded_2(cells, sides, width):
    for axis, dim in sides:
        count = lax.axis_size(axis)
        ends = count - 1
        head = lax.slice_in_dim(cells, 0, width, axis=dim)
        tail = lax.slice_in_dim(cells, cells.shape[dim] - width, cells.shape[dim], axis=dim)
        cells = jnp.concatenate(
            [
                lax.ppermute(tail, axis, [(i, (i + 1) % count) for i in range(ends)]),
                cells,
                lax.ppermute(head, axis, [((i + 1) % count, i) for i in range(ends)]),
            ],
            axis=dim,
        )
    return cells


def two_products(residual, image):
    return (
        one_axis_at_a_time(jnp.sum(residual * residual), GZ_XY),
        one_axis_at_a_time(jnp.sum(residual * image), GZ_XY),
    )


def body(
    right_side,
    stiff_across,
    stiff_down,
    anchor,
    source_node,
    target_cell,
    corner_weight,
    block_count,
):
    rows = stiff_across.shape[1]
    cols = stiff_across.shape[2]
    rhs = right_side[:, 0]
    across = stiff_across[0]
    down = stiff_down[0]
    hold = anchor[0]
    source = source_node[0, 0]
    target = target_cell[0, 0]
    weights = corner_weight[:, 0, 0]
    count = block_count[0, 0]
    slots = source.shape[0]
    has_next = lax.axis_index(GZ) < lax.axis_size(GZ) - 1
    live = ((jnp.arange(slots, dtype=jnp.int32) < count * BLOCK) & has_next).astype(jnp.float32)
    offsets = jnp.array([0, 1, cols, cols + 1], dtype=jnp.int32)
    corners = target[None, :] + offsets[:, None]
    rim = passed_along(down[-1:, :], XY, 1)
    down_above = jnp.concatenate([rim, down[:-1]], 0)
    across_left = jnp.concatenate([jnp.zeros((rows, 1), jnp.float32), across[:, :-1]], 1)
    got_corners = passed_along(corners, GZ, 1)
    got_weights = passed_along(weights, GZ, 1)

    def springs(field):
        padded = padded_2(field, ((XY, 1),), 1)
        upper = padded[:, :-2]
        lower = padded[:, 2:]
        zero_col = jnp.zeros((2, rows, 1), jnp.float32)
        right = jnp.concatenate([field[:, :, 1:], zero_col], 2)
        left = jnp.concatenate([zero_col, field[:, :, :-1]], 2)
        return (
            across * (field - right)
            + across_left * (field - left)
            + down * (field - lower)
            + down_above * (field - upper)
            + hold * field
        )

    def links(field):
        flat = field.reshape(2, rows * cols)
        own_values = flat[:, source]
        empty = jnp.zeros((2, rows * cols), jnp.float32)
        interp_mine = jnp.sum(got_weights[None] * flat[:, got_corners], 1)
        interp = passed_along(interp_mine, GZ, -1)
        error = (interp - own_values) * live[None]
        error_in = passed_along(error, GZ, 1)
        onward = empty.at[:, got_corners.reshape(-1)].add(
            (got_weights[None] * error_in[:, None, :]).reshape(2, -1)
        )
        own = empty.at[:, source].add(-error)
        return (own + onward).reshape(2, rows, cols)

    def operate(field):
        return springs(field) + links(field)

    solution_field = jnp.zeros_like(rhs)
    residual = rhs
    image = operate(residual)
    norm_now, product = two_products(residual, image)
    alpha = norm_now / product
    direction, along = (residual, image)
    for step in range(ITERS):
        solution_field = solution_field + alpha * direction
        residual = residual - alpha * along
        if step + 1 < ITERS:
            image = operate(residual)
            norm_next, product = two_products(residual, image)
            ratio = norm_next / norm_now
            alpha = norm_next / (product - ratio * norm_next / alpha)
            direction = residual + ratio * direction
            along = image + ratio * along
            norm_now = norm_next
    return (solution_field[:, None], residual[:, None])


def solution(mesh):
    split = Mesh(mesh.devices.reshape(4, 16, 4, 2), ("gz_0", "gz_1", "xy_0", "xy_1"))
    in_specs = (
        P(None, GZ, XY, None),
        P(GZ, XY, None),
        P(GZ, XY, None),
        P(GZ, XY, None),
        P(GZ, XY, None),
        P(GZ, XY, None),
        P(None, GZ, XY, None),
        P(GZ, XY),
    )
    out_specs = (P(None, GZ, XY, None), P(None, GZ, XY, None))
    return jax.shard_map(body, mesh=split, in_specs=in_specs, out_specs=out_specs, check_vma=False)
```

profile of v0, /device:TPU:1, one launch (start us, length us, event | category | flops | bytes accessed | tf_op | source)
XLA Modules:
  0.0 437.8 jit_solution(2395866498176098867)
XLA Ops:
  23.8 5.5 %copy.51 = f32[2,1,8,2048]{0,3,2,1:T(8,128)} copy(f32[2,1,8,2048]{3,2,1,0:T(8,128)} %param.9) | data formatting | bytes 262144 | tf_op args[0]
  29.3 6.2 %gather_fusion.1 = f32[1024,2]{1,0:T(8,128)S(1)} fusion(f32[2,16384]{0,1:T(8,128)} %bitcast.83, s32[1024]{0:T(1024)S(1)} %broadcast_clamp_fusion), kind=kCustom, calls=%fused_computation.1 | custom fusion | bytes 20480 | tf_op jit(solution)/shard_map/gather | solution.py:98
  35.8 14.1 %gather_fusion = f32[4096,2]{1,0:T(8,128)S(1)} fusion(f32[2,16384]{0,1:T(8,128)} %bitcast.84, s32[4096]{0:T(1024)S(1)} %bitcast_clamp_fusion), kind=kCustom, calls=%fused_computation | custom fusion | bytes 81920 | tf_op jit(solution)/shard_map/gather | solution.py:100
  62.0 38.0 %scatter_custom_fusion = f32[2,16384]{0,1:T(8,128)} fusion(s32[5120]{0:T(1024)S(1)} %bitcast.115, f32[5120,2]{1,0:T(8,128)S(1)} %copy.54, f32[]{:T(128)} %constant.10.clone.1), kind=kCustom, calls=%fused_computation.13 | custom fusion | flops 10240 | bytes 131076 | tf_op jit(solution)/shard_map/add | solution.py:108
  100.0 5.3 %copy.55 = f32[2,8,2048]{2,1,0:T(8,128)S(1)} copy(f32[2,8,2048]{0,2,1:T(8,128)} %bitcast.81) | data formatting | bytes 262144 | tf_op jit(solution)/shard_map/reshape | solution.py:108
  106.0 8.1 %all-reduce.15 = (f32[]{:T(128)}, f32[]{:T(128)}) all-reduce(f32[]{:T(128)} %get-tuple-element.7, f32[]{:T(128)} %get-tuple-element.6), channel_id=1, replica_groups=mesh['gz_0'=4,'gz_1'=16,'xy_0'=4,'xy_1'=2] {'gz_0'}, use_global_device_ids=true, to_apply=%region_1.0 | all-reduce | flops 2 | bytes 16 | tf_op jit(solution)/shard_map/psum | solution.py:16
  114.1 21.8 %all-reduce.9 = (f32[]{:T(128)}, f32[]{:T(128)}) all-reduce(f32[]{:T(128)} %get-tuple-element.24, f32[]{:T(128)} %get-tuple-element.25), channel_id=1, replica_groups=mesh['gz_0'=4,'gz_1'=16,'xy_0'=4,'xy_1'=2] {'gz_1'}, use_global_device_ids=true, to_apply=%region_2.0 | all-reduce | flops 2 | bytes 16 | tf_op jit(solution)/shard_map/psum | solution.py:16
  135.9 7.8 %all-reduce.12 = (f32[]{:T(128)}, f32[]{:T(128)}) all-reduce(f32[]{:T(128)} %get-tuple-element.12, f32[]{:T(128)} %get-tuple-element.13), channel_id=1, replica_groups=mesh['gz_0'=4,'gz_1'=16,'xy_0'=4,'xy_1'=2] {'xy_0'}, use_global_device_ids=true, to_apply=%region_3.0 | all-reduce | flops 2 | bytes 16 | tf_op jit(solution)/shard_map/psum | solution.py:16
  143.8 16.2 %all-reduce.18 = (f32[]{:T(128)}, f32[]{:T(128)}) all-reduce(f32[]{:T(128)} %get-tuple-element.18, f32[]{:T(128)} %get-tuple-element.19), channel_id=1, replica_groups=mesh['gz_0'=4,'gz_1'=16,'xy_0'=4,'xy_1'=2] {'xy_1'}, use_global_device_ids=true, to_apply=%region_4.0 | all-reduce | flops 2 | bytes 16 | tf_op jit(solution)/shard_map/psum | solution.py:16
  165.9 14.1 %gather_fusion.2 = f32[4096,2]{1,0:T(8,128)S(1)} fusion(f32[2,16384]{0,1:T(8,128)} %bitcast.87, s32[4096]{0:T(1024)S(1)} %bitcast_clamp_fusion), kind=kCustom, calls=%fused_computation.2 | custom fusion | bytes 81920 | tf_op jit(solution)/shard_map/gather | solution.py:100
  183.1 6.2 %gather_fusion.3 = f32[1024,2]{1,0:T(8,128)S(1)} fusion(f32[2,16384]{0,1:T(8,128)} %bitcast.88, s32[1024]{0:T(1024)S(1)} %copy-done.13), kind=kCustom, calls=%fused_computation.3 | custom fusion | bytes 20480 | tf_op jit(solution)/shard_map/gather | solution.py:98
  200.0 38.1 %scatter_custom_fusion.1 = f32[2,16384]{0,1:T(8,128)} fusion(s32[5120]{0:T(1024)} %bitcast.116, f32[5120,2]{1,0:T(8,128)S(1)} %copy.59, f32[]{:T(128)} %constant.10.clone.1), kind=kCustom, calls=%fused_computation.11 | custom fusion | flops 10240 | bytes 131584 | tf_op jit(solution)/shard_map/add | solution.py:108
  245.5 6.7 %all-reduce.14 = (f32[]{:T(128)}, f32[]{:T(128)}) all-reduce(f32[]{:T(128)} %get-tuple-element.5, f32[]{:T(128)} %get-tuple-element.4), channel_id=1, replica_groups=mesh['gz_0'=4,'gz_1'=16,'xy_0'=4,'xy_1'=2] {'gz_0'}, use_global_device_ids=true, to_apply=%region_13.0 | all-reduce | flops 2 | bytes 16 | tf_op jit(solution)/shard_map/psum | solution.py:16
  252.3 20.7 %all-reduce.8 = (f32[]{:T(128)}, f32[]{:T(128)}) all-reduce(f32[]{:T(128)} %get-tuple-element.22, f32[]{:T(128)} %get-tuple-element.23), channel_id=1, replica_groups=mesh['gz_0'=4,'gz_1'=16,'xy_0'=4,'xy_1'=2] {'gz_1'}, use_global_device_ids=true, to_apply=%region_14.0 | all-reduce | flops 2 | bytes 16 | tf_op jit(solution)/shard_map/psum | solution.py:16
  272.9 6.9 %all-reduce.11 = (f32[]{:T(128)}, f32[]{:T(128)}) all-reduce(f32[]{:T(128)} %get-tuple-element.10, f32[]{:T(128)} %get-tuple-element.11), channel_id=1, replica_groups=mesh['gz_0'=4,'gz_1'=16,'xy_0'=4,'xy_1'=2] {'xy_0'}, use_global_device_ids=true, to_apply=%region_15.0 | all-reduce | flops 2 | bytes 16 | tf_op jit(solution)/shard_map/psum | solution.py:16
  279.8 13.2 %all-reduce.17 = (f32[]{:T(128)}, f32[]{:T(128)}) all-reduce(f32[]{:T(128)} %get-tuple-element.16, f32[]{:T(128)} %get-tuple-element.17), channel_id=1, replica_groups=mesh['gz_0'=4,'gz_1'=16,'xy_0'=4,'xy_1'=2] {'xy_1'}, use_global_device_ids=true, to_apply=%region_16.0 | all-reduce | flops 2 | bytes 16 | tf_op jit(solution)/shard_map/psum | solution.py:16
  302.3 14.1 %gather_fusion.4 = f32[4096,2]{1,0:T(8,128)S(1)} fusion(f32[2,16384]{0,1:T(8,128)} %bitcast.85, s32[4096]{0:T(1024)S(1)} %bitcast_clamp_fusion), kind=kCustom, calls=%fused_computation.4 | custom fusion | bytes 81920 | tf_op jit(solution)/shard_map/gather | solution.py:100
  319.4 6.7 %gather_fusion.5 = f32[1024,2]{1,0:T(8,128)S(1)} fusion(f32[2,16384]{0,1:T(8,128)} %bitcast.86, s32[1024]{0:T(1024)} %copy-done.12), kind=kCustom, calls=%fused_computation.5 | custom fusion | bytes 20480 | tf_op jit(solution)/shard_map/gather | solution.py:98
  340.4 38.1 %scatter_custom_fusion.2 = f32[2,16384]{0,1:T(8,128)} fusion(s32[5120]{0:T(1024)} %bitcast.117, f32[5120,2]{1,0:T(8,128)S(1)} %copy.64, f32[]{:T(128)} %constant.10.clone.1), kind=kCustom, calls=%fused_computation.9 | custom fusion | flops 10240 | bytes 131584 | tf_op jit(solution)/shard_map/add | solution.py:108
  378.5 5.3 %copy.65 = f32[2,8,2048]{2,1,0:T(8,128)S(1)} copy(f32[2,8,2048]{0,2,1:T(8,128)} %bitcast.80) | data formatting | bytes 262144 | tf_op jit(solution)/shard_map/reshape | solution.py:108
  385.3 6.6 %all-reduce.13 = (f32[]{:T(128)}, f32[]{:T(128)}) all-reduce(f32[]{:T(128)} %get-tuple-element.3, f32[]{:T(128)} %get-tuple-element.2), channel_id=1, replica_groups=mesh['gz_0'=4,'gz_1'=16,'xy_0'=4,'xy_1'=2] {'gz_0'}, use_global_device_ids=true, to_apply=%region_25.0 | all-reduce | flops 2 | bytes 16 | tf_op jit(solution)/shard_map/psum | solution.py:16
  391.9 21.0 %all-reduce.7 = (f32[]{:T(128)}, f32[]{:T(128)}) all-reduce(f32[]{:T(128)} %get-tuple-element.20, f32[]{:T(128)} %get-tuple-element.21), channel_id=1, replica_groups=mesh['gz_0'=4,'gz_1'=16,'xy_0'=4,'xy_1'=2] {'gz_1'}, use_global_device_ids=true, to_apply=%region_26.0 | all-reduce | flops 2 | bytes 16 | tf_op jit(solution)/shard_map/psum | solution.py:16
  412.9 7.3 %all-reduce.10 = (f32[]{:T(128)}, f32[]{:T(128)}) all-reduce(f32[]{:T(128)} %get-tuple-element.8, f32[]{:T(128)} %get-tuple-element.9), channel_id=1, replica_groups=mesh['gz_0'=4,'gz_1'=16,'xy_0'=4,'xy_1'=2] {'xy_0'}, use_global_device_ids=true, to_apply=%region_27.0 | all-reduce | flops 2 | bytes 16 | tf_op jit(solution)/shard_map/psum | solution.py:16
  420.2 12.8 %all-reduce.16 = (f32[]{:T(128)}, f32[]{:T(128)}) all-reduce(f32[]{:T(128)} %get-tuple-element.14, f32[]{:T(128)} %get-tuple-element.15), channel_id=1, replica_groups=mesh['gz_0'=4,'gz_1'=16,'xy_0'=4,'xy_1'=2] {'xy_1'}, use_global_device_ids=true, to_apply=%region_28.0 | all-reduce | flops 2 | bytes 16 | tf_op jit(solution)/shard_map/psum | solution.py:16
  (121 shorter events, 85.0 us)
Async XLA Ops:
  1.4 34.4 %collective-permute-start.3 = (s32[4,1024]{1,0:T(4,128)S(1)}, s32[4,1024]{1,0:T(4,128)S(1)}, u32[]{:S(2)}, u32[]{:S(2)}) collective-permute-start(s32[4,1024]{1,0:T(4,128)S(1)} %broadcast_add_fusion), channel_id=1, source_target_pairs={{0,8},{8,16},{16,24},{24,32},{32,40},{40,48},{48,56},{56,64},{64,7... | collective-permute-start | bytes 49160 | tf_op jit(solution)/shard_map/ppermute | solution.py:23
  6.5 43.5 %collective-permute-start.4 = (f32[4,1024]{1,0:T(4,128)S(1)}, f32[4,1024]{1,0:T(4,128)S(1)}, u32[]{:S(2)}, u32[]{:S(2)}) collective-permute-start(f32[4,1024]{1,0:T(4,128)S(1)} %bitcast.118), channel_id=1, source_target_pairs={{0,8},{8,16},{16,24},{24,32},{32,40},{40,48},{48,56},{56,64},{64,7... | collective-permute-start | bytes 49160 | tf_op jit(solution)/shard_map/ppermute | solution.py:23
  11.1 94.2 %collective-permute-start = (f32[2,1,2048]{2,1,0:T(1,128)S(1)}, f32[2,1,2048]{2,1,0:T(1,128)S(1)}, u32[]{:S(2)}, u32[]{:S(2)}) collective-permute-start(f32[2,1,2048]{2,1,0:T(1,128)S(1)} %get-tuple-element.53), channel_id=1, source_target_pairs={{1,0},{2,1},{3,2},{4,3},{5,4},{6,5},{7,6},{9,8},{10,9},{11,10},{12... | collective-permute-start | bytes 49160 | tf_op jit(solution)/shard_map/ppermute | solution.py:36
  14.5 90.7 %collective-permute-start.2 = (f32[2,1,2048]{2,1,0:T(1,128)S(1)}, f32[2,1,2048]{2,1,0:T(1,128)S(1)}, u32[]{:S(2)}, u32[]{:S(2)}) collective-permute-start(f32[2,1,2048]{2,1,0:T(1,128)S(1)} %get-tuple-element.54), channel_id=1, source_target_pairs={{0,1},{1,2},{2,3},{3,4},{4,5},{5,6},{6,7},{8,9},{9,10},{10,11},{11... | collective-permute-start | bytes 49160 | tf_op jit(solution)/shard_map/ppermute | solution.py:34
  18.1 17.7 %collective-permute-start.1 = (f32[1,2048]{1,0:T(1,128)S(1)}, f32[1,2048]{1,0:T(1,128)S(1)}, u32[]{:S(2)}, u32[]{:S(2)}) collective-permute-start(f32[1,2048]{1,0:T(1,128)S(1)} %slice_bitcast_fusion.1), channel_id=1, source_target_pairs={{0,1},{1,2},{2,3},{3,4},{4,5},{5,6},{6,7},{8,9},{9,10},{10,11},{11... | collective-permute-start | bytes 24584 | tf_op jit(solution)/shard_map/ppermute | solution.py:23
  23.1 6.2 %copy-start.12 = (s32[1024]{0:T(1024)}, s32[1024]{0:T(1024)S(1)}, u32[]{:S(2)}) copy-start(s32[1024]{0:T(1024)S(1)} %broadcast_clamp_fusion) | copy-start | bytes 12292
  23.8 31.7 %copy-start.10 = (f32[1024]{0:T(1024)}, f32[1024]{0:T(1024)S(1)}, u32[]{:S(2)}) copy-start(f32[1024]{0:T(1024)S(1)} %fusion.35) | copy-start | bytes 12292
  23.8 11.9 %copy-start.2 = (f32[1,8,2048]{2,1,0:T(8,128)S(1)}, f32[1,8,2048]{2,1,0:T(8,128)}, u32[]{:S(2)}) copy-start(f32[1,8,2048]{2,1,0:T(8,128)} %param.10) | copy-start | bytes 196612
  50.9 4.6 %collective-permute-start.5 = (f32[2,1024]{1,0:T(2,128)S(1)}, f32[2,1024]{1,0:T(2,128)S(1)}, u32[]{:S(2)}, u32[]{:S(2)}) collective-permute-start(f32[2,1024]{1,0:T(2,128)S(1)} %bitcast.121), channel_id=1, source_target_pairs={{8,0},{16,8},{24,16},{32,24},{40,32},{48,40},{56,48},{64,56},{72,6... | collective-permute-start | bytes 24584 | tf_op jit(solution)/shard_map/ppermute | solution.py:23
  55.5 5.5 %collective-permute-start.6 = (f32[2,1024]{1,0:T(2,128)S(1)}, f32[2,1024]{1,0:T(2,128)S(1)}, u32[]{:S(2)}, u32[]{:S(2)}) collective-permute-start(f32[2,1024]{1,0:T(2,128)S(1)} %get-tuple-element.40), channel_id=1, source_target_pairs={{0,8},{8,16},{16,24},{24,32},{32,40},{40,48},{48,56},{56,64},{64,7... | collective-permute-start | bytes 24584 | tf_op jit(solution)/shard_map/ppermute | solution.py:23
  60.3 39.6 %copy-start.14 = (s32[5120,1]{0,1:T(1,128)}, s32[5120,1]{0,1:T(1,128)S(1)}, u32[]{:S(2)}) copy-start(s32[5120,1]{0,1:T(1,128)S(1)} %pad_add_fusion) | copy-start | bytes 61444
  60.3 138.8 %copy-start.9 = (f32[1,8,4,128]{3,1,2,0:T(8,128)}, f32[1,8,4,128]{3,1,2,0:T(8,128)S(1)}, u32[]{:S(2)}) copy-start(f32[1,8,4,128]{3,1,2,0:T(8,128)S(1)} %copy.76) | copy-start | bytes 49156
  165.9 17.1 %copy-start.13 = (s32[1024]{0:T(1024)S(1)}, s32[1024]{0:T(1024)}, u32[]{:S(2)}) copy-start(s32[1024]{0:T(1024)} %copy-done.12) | copy-start | bytes 12292
  165.9 23.5 %copy-start.11 = (f32[1024]{0:T(1024)S(1)}, f32[1024]{0:T(1024)}, u32[]{:S(2)}) copy-start(f32[1024]{0:T(1024)} %copy-done.10) | copy-start | bytes 12292
  181.0 8.4 %collective-permute-start.9 = (f32[2,1024]{1,0:T(2,128)S(1)}, f32[2,1024]{1,0:T(2,128)S(1)}, u32[]{:S(2)}, u32[]{:S(2)}) collective-permute-start(f32[2,1024]{1,0:T(2,128)S(1)} %bitcast.120), channel_id=1, source_target_pairs={{8,0},{16,8},{24,16},{32,24},{40,32},{48,40},{56,48},{64,56},{72,6... | collective-permute-start | bytes 24584 | tf_op jit(solution)/shard_map/ppermute | solution.py:23
  189.5 9.6 %collective-permute-start.10 = (f32[2,1024]{1,0:T(2,128)S(1)}, f32[2,1024]{1,0:T(2,128)S(1)}, u32[]{:S(2)}, u32[]{:S(2)}) collective-permute-start(f32[2,1024]{1,0:T(2,128)S(1)} %get-tuple-element.37), channel_id=1, source_target_pairs={{0,8},{8,16},{16,24},{24,32},{32,40},{40,48},{48,56},{56,64},{64,7... | collective-permute-start | bytes 24584 | tf_op jit(solution)/shard_map/ppermute | solution.py:23
  193.5 49.9 %collective-permute-start.7 = (f32[2,1,2048]{2,1,0:T(1,128)S(1)}, f32[2,1,2048]{2,1,0:T(1,128)S(1)}, u32[]{:S(2)}, u32[]{:S(2)}) collective-permute-start(f32[2,1,2048]{2,1,0:T(1,128)S(1)} %get-tuple-element.49), channel_id=1, source_target_pairs={{1,0},{2,1},{3,2},{4,3},{5,4},{6,5},{7,6},{9,8},{10,9},{11,10},{12... | collective-permute-start | bytes 49160 | tf_op jit(solution)/shard_map/ppermute | solution.py:36
  196.3 47.1 %collective-permute-start.8 = (f32[2,1,2048]{2,1,0:T(1,128)S(1)}, f32[2,1,2048]{2,1,0:T(1,128)S(1)}, u32[]{:S(2)}, u32[]{:S(2)}) collective-permute-start(f32[2,1,2048]{2,1,0:T(1,128)S(1)} %get-tuple-element.50), channel_id=1, source_target_pairs={{0,1},{1,2},{2,3},{3,4},{4,5},{5,6},{6,7},{8,9},{9,10},{10,11},{11... | collective-permute-start | bytes 49160 | tf_op jit(solution)/shard_map/ppermute | solution.py:34
  238.1 5.9 %copy-start.7 = (f32[2,8,2047]{2,1,0:T(8,128)S(1)}, f32[2,8,2047]{2,1,0:T(8,128)}, u32[]{:S(2)}) copy-start(f32[2,8,2047]{2,1,0:T(8,128)} %get-tuple-element.47) | copy-start | bytes 393028
  238.1 5.9 %copy-start.8 = (f32[2,8,2047]{2,1,0:T(8,128)S(1)}, f32[2,8,2047]{2,1,0:T(8,128)}, u32[]{:S(2)}) copy-start(f32[2,8,2047]{2,1,0:T(8,128)} %get-tuple-element.48) | copy-start | bytes 393028
  317.3 8.9 %collective-permute-start.13 = (f32[2,1024]{1,0:T(2,128)S(1)}, f32[2,1024]{1,0:T(2,128)S(1)}, u32[]{:S(2)}, u32[]{:S(2)}) collective-permute-start(f32[2,1024]{1,0:T(2,128)S(1)} %bitcast.119), channel_id=1, source_target_pairs={{8,0},{16,8},{24,16},{32,24},{40,32},{48,40},{56,48},{64,56},{72,6... | collective-permute-start | bytes 24584 | tf_op jit(solution)/shard_map/ppermute | solution.py:23
  327.0 10.5 %collective-permute-start.14 = (f32[2,1024]{1,0:T(2,128)S(1)}, f32[2,1024]{1,0:T(2,128)S(1)}, u32[]{:S(2)}, u32[]{:S(2)}) collective-permute-start(f32[2,1024]{1,0:T(2,128)S(1)} %get-tuple-element.34), channel_id=1, source_target_pairs={{0,8},{8,16},{16,24},{24,32},{32,40},{40,48},{48,56},{56,64},{64,7... | collective-permute-start | bytes 24584 | tf_op jit(solution)/shard_map/ppermute | solution.py:23
  331.9 51.9 %collective-permute-start.11 = (f32[2,1,2048]{2,1,0:T(1,128)}, f32[2,1,2048]{2,1,0:T(1,128)S(1)}, u32[]{:S(2)}, u32[]{:S(2)}) collective-permute-start(f32[2,1,2048]{2,1,0:T(1,128)} %get-tuple-element.45), channel_id=1, source_target_pairs={{1,0},{2,1},{3,2},{4,3},{5,4},{6,5},{7,6},{9,8},{10,9},{11,10},{12... | collective-permute-start | bytes 49160 | tf_op jit(solution)/shard_map/ppermute | solution.py:36
  334.4 49.4 %collective-permute-start.12 = (f32[2,1,2048]{2,1,0:T(1,128)}, f32[2,1,2048]{2,1,0:T(1,128)}, u32[]{:S(2)}, u32[]{:S(2)}) collective-permute-start(f32[2,1,2048]{2,1,0:T(1,128)} %get-tuple-element.46), channel_id=1, source_target_pairs={{0,1},{1,2},{2,3},{3,4},{4,5},{5,6},{6,7},{8,9},{9,10},{10,11},{11... | collective-permute-start | bytes 49160 | tf_op jit(solution)/shard_map/ppermute | solution.py:34
  (8 other events, 33.1 us)
where the time goes:
time: 440 us; the launch traced here: 438 us
  blocking collectives  149 us (34%)
  other arithmetic  125 us (28%)
  local copies, waits for them, and re-layouts  104 us (24%)
  starting transfers between devices  44.4 us (10%)
  between operations  11.8 us (3%)
    psum x12, blocking collectives, one_axis_at_a_time(): shard = lax.psum(shard, axis)  149 us
    add x3, other arithmetic, links(): return (own + onward).reshape(2, rows, cols)  114 us
    gather x3, local copies, waits for them, and re-layouts, links(): interp_mine = jnp.sum(got_weights[None] * flat[:, got_corners], 1)  42.4 us
    ppermute x9, starting transfers between devices, passed_along(): return lax.ppermute(block, axis, route)  27.2 us
    gather x6, local copies, waits for them, and re-layouts, links(): own_values = flat[:, source]  19.6 us
    reshape x3, local copies, waits for them, and re-layouts, links(): return (own + onward).reshape(2, rows, cols)  15.8 us
    sub x2, local copies, waits for them, and re-layouts, body(): residual = residual - alpha * along  9.15 us
  transfers between devices with their start and end apart: 15, of which 2 were waited for; matrix products, arithmetic and copies ran while one was open for 42% of the time, Pallas kernels for 0%

commit v1 on v0

--- a/solution.py
+++ b/solution.py
@@ -13,7 +13,7 @@
 
 def one_axis_at_a_time(shard, axes):
     for axis in axes:
-        shard = lax.psum(shard, axis)
+        shard = jnp.sum(lax.all_gather(shard, axis), axis=0)
     return shard
 
 

time: 440 us -> 486 us (1.10)
  local copies, waits for them, and re-layouts: 104 us -> 142 us
  other arithmetic: 125 us -> 139 us
  blocking collectives: 149 us -> 141 us
    psum x12 -> x0, blocking collectives: 149 us -> none  [one_axis_at_a_time(): shard = lax.psum(shard, axis)]
    unnamed x0 -> x12, blocking collectives: none -> 141 us
    unnamed x44 -> x96, local copies, waits for them, and re-layouts: 6.98 us -> 45.7 us
    reduce_sum x0 -> x24, other arithmetic: none -> 14.6 us  [one_axis_at_a_time(): shard = jnp.sum(lax.all_gather(shard, axis), axis=0)]
  transfers between devices with their start and end apart: 15 -> 15, of which waited for: 2 -> 2; matrix products, arithmetic and copies ran while one was open for 42% -> 38% of each run, Pallas kernels for 0% -> 0%
where the time goes in v1:
time: 486 us; the launch traced here: 484 us
  local copies, waits for them, and re-layouts  142 us (29%)
  blocking collectives  141 us (29%)
  other arithmetic  139 us (29%)
  starting transfers between devices  44.6 us (9%)
  between operations  12.1 us (2%)
    unnamed x12, blocking collectives  141 us
    add x3, other arithmetic, links(): return (own + onward).reshape(2, rows, cols)  114 us
    unnamed x96, local copies, waits for them, and re-layouts  45.7 us
    gather x3, local copies, waits for them, and re-layouts, links(): interp_mine = jnp.sum(got_weights[None] * flat[:, got_corners], 1)  42.4 us
    ppermute x9, starting transfers between devices, passed_along(): return lax.ppermute(block, axis, route)  27.2 us
    gather x6, local copies, waits for them, and re-layouts, links(): own_values = flat[:, source]  19.6 us
    reshape x3, local copies, waits for them, and re-layouts, links(): return (own + onward).reshape(2, rows, cols)  15.8 us
    reduce_sum x24, other arithmetic, one_axis_at_a_time(): shard = jnp.sum(lax.all_gather(shard, axis), axis=0)  14.6 us
  transfers between devices with their start and end apart: 15, of which 2 were waited for; matrix products, arithmetic and copies ran while one was open for 38% of the time, Pallas kernels for 0%

profile of v1, /device:TPU:1, one launch (start us, length us, event | category | flops | bytes accessed | tf_op | source)
XLA Modules:
  0.0 483.8 jit_solution(16346929612817634782)
XLA Ops:
  23.8 5.5 %copy.51 = f32[2,1,8,2048]{0,3,2,1:T(8,128)} copy(f32[2,1,8,2048]{3,2,1,0:T(8,128)} %param.9) | data formatting | bytes 262144 | tf_op args[0]
  29.3 6.2 %gather_fusion.1 = f32[1024,2]{1,0:T(8,128)S(1)} fusion(f32[2,16384]{0,1:T(8,128)} %bitcast.111, s32[1024]{0:T(1024)S(1)} %broadcast_clamp_fusion), kind=kCustom, calls=%fused_computation.1 | custom fusion | bytes 20480 | tf_op jit(solution)/shard_map/gather | solution.py:98
  38.5 14.1 %gather_fusion = f32[4096,2]{1,0:T(8,128)S(1)} fusion(f32[2,16384]{0,1:T(8,128)} %bitcast.112, s32[4096]{0:T(1024)S(1)} %bitcast_clamp_fusion), kind=kCustom, calls=%fused_computation | custom fusion | bytes 81920 | tf_op jit(solution)/shard_map/gather | solution.py:100
  64.6 38.0 %scatter_custom_fusion = f32[2,16384]{0,1:T(8,128)} fusion(s32[5120]{0:T(1024)S(1)} %bitcast.143, f32[5120,2]{1,0:T(8,128)S(1)} %copy.54, f32[]{:T(128)} %constant.10.clone.1), kind=kCustom, calls=%fused_computation.13 | custom fusion | flops 10240 | bytes 131076 | tf_op jit(solution)/shard_map/add | solution.py:108
  102.6 5.3 %copy.55 = f32[2,8,2048]{2,1,0:T(8,128)S(1)} copy(f32[2,8,2048]{0,2,1:T(8,128)} %bitcast.109) | data formatting | bytes 262144 | tf_op jit(solution)/shard_map/reshape | solution.py:108
  112.7 7.4 %all-reduce.39 = (f32[4]{0:T(128)S(1)}, f32[4]{0:T(128)S(1)}) all-reduce(f32[4]{0:T(128)S(1)} %dynamic-update-slice, f32[4]{0:T(128)S(1)} %dynamic-update-slice.4), channel_id=1, replica_groups=mesh['gz_0'=4,'gz_1'=16,'xy_0'=4,'xy_1'=2] {'gz_0'}, use_global_device_ids=true, to_apply=%add.7 | all-reduce | flops 8 | bytes 64
  124.1 21.2 %all-reduce.33 = (f32[16]{0:T(128)S(1)}, f32[16]{0:T(128)S(1)}) all-reduce(f32[16]{0:T(128)S(1)} %dynamic-update-slice.1, f32[16]{0:T(128)S(1)} %dynamic-update-slice.5), channel_id=1, replica_groups=mesh['gz_0'=4,'gz_1'=16,'xy_0'=4,'xy_1'=2] {'gz_1'}, use_global_device_ids=true, to_apply=%add.8 | all-reduce | flops 32 | bytes 256
  150.7 7.2 %all-reduce.36 = (f32[4]{0:T(128)S(1)}, f32[4]{0:T(128)S(1)}) all-reduce(f32[4]{0:T(128)S(1)} %dynamic-update-slice.2, f32[4]{0:T(128)S(1)} %dynamic-update-slice.6), channel_id=1, replica_groups=mesh['gz_0'=4,'gz_1'=16,'xy_0'=4,'xy_1'=2] {'xy_0'}, use_global_device_ids=true, to_apply=%add.9 | all-reduce | flops 8 | bytes 64
  161.9 15.5 %all-reduce.42 = (f32[2]{0:T(128)S(1)}, f32[2]{0:T(128)S(1)}) all-reduce(f32[2]{0:T(128)S(1)} %dynamic-update-slice.3, f32[2]{0:T(128)S(1)} %dynamic-update-slice.7), channel_id=1, replica_groups=mesh['gz_0'=4,'gz_1'=16,'xy_0'=4,'xy_1'=2] {'xy_1'}, use_global_device_ids=true, to_apply=%add.10 | all-reduce | flops 4 | bytes 32
  184.7 14.1 %gather_fusion.2 = f32[4096,2]{1,0:T(8,128)S(1)} fusion(f32[2,16384]{0,1:T(8,128)} %bitcast.115, s32[4096]{0:T(1024)S(1)} %bitcast_clamp_fusion), kind=kCustom, calls=%fused_computation.2 | custom fusion | bytes 81920 | tf_op jit(solution)/shard_map/gather | solution.py:100
  201.8 6.2 %gather_fusion.3 = f32[1024,2]{1,0:T(8,128)S(1)} fusion(f32[2,16384]{0,1:T(8,128)} %bitcast.116, s32[1024]{0:T(1024)S(1)} %copy-done.13), kind=kCustom, calls=%fused_computation.3 | custom fusion | bytes 20480 | tf_op jit(solution)/shard_map/gather | solution.py:98
  218.9 38.1 %scatter_custom_fusion.1 = f32[2,16384]{0,1:T(8,128)} fusion(s32[5120]{0:T(1024)} %bitcast.144, f32[5120,2]{1,0:T(8,128)S(1)} %copy.59, f32[]{:T(128)} %constant.10.clone.1), kind=kCustom, calls=%fused_computation.11 | custom fusion | flops 10240 | bytes 131584 | tf_op jit(solution)/shard_map/add | solution.py:108
  267.2 6.1 %all-reduce.38 = (f32[4]{0:T(128)S(1)}, f32[4]{0:T(128)S(1)}) all-reduce(f32[4]{0:T(128)S(1)} %dynamic-update-slice.8, f32[4]{0:T(128)S(1)} %dynamic-update-slice.12), channel_id=1, replica_groups=mesh['gz_0'=4,'gz_1'=16,'xy_0'=4,'xy_1'=2] {'gz_0'}, use_global_device_ids=true, to_apply=%add.15 | all-reduce | flops 8 | bytes 64
  277.3 20.0 %all-reduce.32 = (f32[16]{0:T(128)S(1)}, f32[16]{0:T(128)S(1)}) all-reduce(f32[16]{0:T(128)S(1)} %dynamic-update-slice.9, f32[16]{0:T(128)S(1)} %dynamic-update-slice.13), channel_id=1, replica_groups=mesh['gz_0'=4,'gz_1'=16,'xy_0'=4,'xy_1'=2] {'gz_1'}, use_global_device_ids=true, to_apply=%add.16 | all-reduce | flops 32 | bytes 256
  301.4 6.3 %all-reduce.35 = (f32[4]{0:T(128)S(1)}, f32[4]{0:T(128)S(1)}) all-reduce(f32[4]{0:T(128)S(1)} %dynamic-update-slice.10, f32[4]{0:T(128)S(1)} %dynamic-update-slice.14), channel_id=1, replica_groups=mesh['gz_0'=4,'gz_1'=16,'xy_0'=4,'xy_1'=2] {'xy_0'}, use_global_device_ids=true, to_apply=%add.17 | all-reduce | flops 8 | bytes 64
  311.6 12.5 %all-reduce.41 = (f32[2]{0:T(128)S(1)}, f32[2]{0:T(128)S(1)}) all-reduce(f32[2]{0:T(128)S(1)} %dynamic-update-slice.11, f32[2]{0:T(128)S(1)} %dynamic-update-slice.15), channel_id=1, replica_groups=mesh['gz_0'=4,'gz_1'=16,'xy_0'=4,'xy_1'=2] {'xy_1'}, use_global_device_ids=true, to_apply=%add.18 | all-reduce | flops 4 | bytes 32
  334.8 14.1 %gather_fusion.4 = f32[4096,2]{1,0:T(8,128)S(1)} fusion(f32[2,16384]{0,1:T(8,128)} %bitcast.113, s32[4096]{0:T(1024)S(1)} %bitcast_clamp_fusion), kind=kCustom, calls=%fused_computation.4 | custom fusion | bytes 81920 | tf_op jit(solution)/shard_map/gather | solution.py:100
  351.9 6.7 %gather_fusion.5 = f32[1024,2]{1,0:T(8,128)S(1)} fusion(f32[2,16384]{0,1:T(8,128)} %bitcast.114, s32[1024]{0:T(1024)} %copy-done.12), kind=kCustom, calls=%fused_computation.5 | custom fusion | bytes 20480 | tf_op jit(solution)/shard_map/gather | solution.py:98
  372.9 38.1 %scatter_custom_fusion.2 = f32[2,16384]{0,1:T(8,128)} fusion(s32[5120]{0:T(1024)} %bitcast.145, f32[5120,2]{1,0:T(8,128)S(1)} %copy.64, f32[]{:T(128)} %constant.10.clone.1), kind=kCustom, calls=%fused_computation.9 | custom fusion | flops 10240 | bytes 131584 | tf_op jit(solution)/shard_map/add | solution.py:108
  411.0 5.3 %copy.65 = f32[2,8,2048]{2,1,0:T(8,128)S(1)} copy(f32[2,8,2048]{0,2,1:T(8,128)} %bitcast.108) | data formatting | bytes 262144 | tf_op jit(solution)/shard_map/reshape | solution.py:108
  420.6 6.0 %all-reduce.37 = (f32[4]{0:T(128)S(1)}, f32[4]{0:T(128)S(1)}) all-reduce(f32[4]{0:T(128)S(1)} %dynamic-update-slice.16, f32[4]{0:T(128)S(1)} %dynamic-update-slice.20), channel_id=1, replica_groups=mesh['gz_0'=4,'gz_1'=16,'xy_0'=4,'xy_1'=2] {'gz_0'}, use_global_device_ids=true, to_apply=%add.23 | all-reduce | flops 8 | bytes 64
  430.5 20.3 %all-reduce.31 = (f32[16]{0:T(128)S(1)}, f32[16]{0:T(128)S(1)}) all-reduce(f32[16]{0:T(128)S(1)} %dynamic-update-slice.17, f32[16]{0:T(128)S(1)} %dynamic-update-slice.21), channel_id=1, replica_groups=mesh['gz_0'=4,'gz_1'=16,'xy_0'=4,'xy_1'=2] {'gz_1'}, use_global_device_ids=true, to_apply=%add.24 | all-reduce | flops 32 | bytes 256
  454.9 6.7 %all-reduce.34 = (f32[4]{0:T(128)S(1)}, f32[4]{0:T(128)S(1)}) all-reduce(f32[4]{0:T(128)S(1)} %dynamic-update-slice.18, f32[4]{0:T(128)S(1)} %dynamic-update-slice.22), channel_id=1, replica_groups=mesh['gz_0'=4,'gz_1'=16,'xy_0'=4,'xy_1'=2] {'xy_0'}, use_global_device_ids=true, to_apply=%add.25 | all-reduce | flops 8 | bytes 64
  465.6 12.2 %all-reduce.40 = (f32[2]{0:T(128)S(1)}, f32[2]{0:T(128)S(1)}) all-reduce(f32[2]{0:T(128)S(1)} %dynamic-update-slice.19, f32[2]{0:T(128)S(1)} %dynamic-update-slice.23), channel_id=1, replica_groups=mesh['gz_0'=4,'gz_1'=16,'xy_0'=4,'xy_1'=2] {'xy_1'}, use_global_device_ids=true, to_apply=%add.26 | all-reduce | flops 4 | bytes 32
  (197 shorter events, 138.5 us)
Async XLA Ops:
  1.4 37.0 %collective-permute-start.3 = (s32[4,1024]{1,0:T(4,128)S(1)}, s32[4,1024]{1,0:T(4,128)S(1)}, u32[]{:S(2)}, u32[]{:S(2)}) collective-permute-start(s32[4,1024]{1,0:T(4,128)S(1)} %broadcast_add_fusion), channel_id=1, source_target_pairs={{0,8},{8,16},{16,24},{24,32},{32,40},{40,48},{48,56},{56,64},{64,7... | collective-permute-start | bytes 49160 | tf_op jit(solution)/shard_map/ppermute | solution.py:23
  6.5 46.1 %collective-permute-start.4 = (f32[4,1024]{1,0:T(4,128)S(1)}, f32[4,1024]{1,0:T(4,128)S(1)}, u32[]{:S(2)}, u32[]{:S(2)}) collective-permute-start(f32[4,1024]{1,0:T(4,128)S(1)} %bitcast.146), channel_id=1, source_target_pairs={{0,8},{8,16},{16,24},{24,32},{32,40},{40,48},{48,56},{56,64},{64,7... | collective-permute-start | bytes 49160 | tf_op jit(solution)/shard_map/ppermute | solution.py:23
  11.1 96.8 %collective-permute-start = (f32[2,1,2048]{2,1,0:T(1,128)S(1)}, f32[2,1,2048]{2,1,0:T(1,128)S(1)}, u32[]{:S(2)}, u32[]{:S(2)}) collective-permute-start(f32[2,1,2048]{2,1,0:T(1,128)S(1)} %get-tuple-element.53), channel_id=1, source_target_pairs={{1,0},{2,1},{3,2},{4,3},{5,4},{6,5},{7,6},{9,8},{10,9},{11,10},{12... | collective-permute-start | bytes 49160 | tf_op jit(solution)/shard_map/ppermute | solution.py:36
  14.5 93.4 %collective-permute-start.2 = (f32[2,1,2048]{2,1,0:T(1,128)S(1)}, f32[2,1,2048]{2,1,0:T(1,128)S(1)}, u32[]{:S(2)}, u32[]{:S(2)}) collective-permute-start(f32[2,1,2048]{2,1,0:T(1,128)S(1)} %get-tuple-element.54), channel_id=1, source_target_pairs={{0,1},{1,2},{2,3},{3,4},{4,5},{5,6},{6,7},{8,9},{9,10},{10,11},{11... | collective-permute-start | bytes 49160 | tf_op jit(solution)/shard_map/ppermute | solution.py:34
  18.1 20.3 %collective-permute-start.1 = (f32[1,2048]{1,0:T(1,128)S(1)}, f32[1,2048]{1,0:T(1,128)S(1)}, u32[]{:S(2)}, u32[]{:S(2)}) collective-permute-start(f32[1,2048]{1,0:T(1,128)S(1)} %slice_bitcast_fusion.1), channel_id=1, source_target_pairs={{0,1},{1,2},{2,3},{3,4},{4,5},{5,6},{6,7},{8,9},{9,10},{10,11},{11... | collective-permute-start | bytes 24584 | tf_op jit(solution)/shard_map/ppermute | solution.py:23
  23.8 5.5 %copy-start.12 = (s32[1024]{0:T(1024)}, s32[1024]{0:T(1024)S(1)}, u32[]{:S(2)}) copy-start(s32[1024]{0:T(1024)S(1)} %broadcast_clamp_fusion) | copy-start | bytes 12292
  23.8 34.3 %copy-start.10 = (f32[1024]{0:T(1024)}, f32[1024]{0:T(1024)S(1)}, u32[]{:S(2)}) copy-start(f32[1024]{0:T(1024)S(1)} %fusion.35) | copy-start | bytes 12292
  23.8 14.5 %copy-start.2 = (f32[1,8,2048]{2,1,0:T(8,128)S(1)}, f32[1,8,2048]{2,1,0:T(8,128)}, u32[]{:S(2)}) copy-start(f32[1,8,2048]{2,1,0:T(8,128)} %param.10) | copy-start | bytes 196612
  53.5 4.6 collective-permute-start.5
  58.2 5.5 %collective-permute-start.6 = (f32[2,1024]{1,0:T(2,128)S(1)}, f32[2,1024]{1,0:T(2,128)S(1)}, u32[]{:S(2)}, u32[]{:S(2)}) collective-permute-start(f32[2,1024]{1,0:T(2,128)S(1)} %get-tuple-element.40), channel_id=1, source_target_pairs={{0,8},{8,16},{16,24},{24,32},{32,40},{40,48},{48,56},{56,64},{64,7... | collective-permute-start | bytes 24584 | tf_op jit(solution)/shard_map/ppermute | solution.py:23
  62.9 39.6 %copy-start.14 = (s32[5120,1]{0,1:T(1,128)}, s32[5120,1]{0,1:T(1,128)S(1)}, u32[]{:S(2)}) copy-start(s32[5120,1]{0,1:T(1,128)S(1)} %pad_add_fusion) | copy-start | bytes 61444
  63.0 155.1 %copy-start.9 = (f32[1,8,4,128]{3,1,2,0:T(8,128)}, f32[1,8,4,128]{3,1,2,0:T(8,128)S(1)}, u32[]{:S(2)}) copy-start(f32[1,8,4,128]{3,1,2,0:T(8,128)S(1)} %copy.76) | copy-start | bytes 49156
  184.7 17.1 %copy-start.13 = (s32[1024]{0:T(1024)S(1)}, s32[1024]{0:T(1024)}, u32[]{:S(2)}) copy-start(s32[1024]{0:T(1024)} %copy-done.12) | copy-start | bytes 12292
  184.7 23.5 %copy-start.11 = (f32[1024]{0:T(1024)S(1)}, f32[1024]{0:T(1024)}, u32[]{:S(2)}) copy-start(f32[1024]{0:T(1024)} %copy-done.10) | copy-start | bytes 12292
  199.7 8.4 %collective-permute-start.9 = (f32[2,1024]{1,0:T(2,128)S(1)}, f32[2,1024]{1,0:T(2,128)S(1)}, u32[]{:S(2)}, u32[]{:S(2)}) collective-permute-start(f32[2,1024]{1,0:T(2,128)S(1)} %bitcast.148), channel_id=1, source_target_pairs={{8,0},{16,8},{24,16},{32,24},{40,32},{48,40},{56,48},{64,56},{72,6... | collective-permute-start | bytes 24584 | tf_op jit(solution)/shard_map/ppermute | solution.py:23
  208.2 9.8 %collective-permute-start.10 = (f32[2,1024]{1,0:T(2,128)S(1)}, f32[2,1024]{1,0:T(2,128)S(1)}, u32[]{:S(2)}, u32[]{:S(2)}) collective-permute-start(f32[2,1024]{1,0:T(2,128)S(1)} %get-tuple-element.37), channel_id=1, source_target_pairs={{0,8},{8,16},{16,24},{24,32},{32,40},{40,48},{48,56},{56,64},{64,7... | collective-permute-start | bytes 24584 | tf_op jit(solution)/shard_map/ppermute | solution.py:23
  212.2 50.1 %collective-permute-start.7 = (f32[2,1,2048]{2,1,0:T(1,128)S(1)}, f32[2,1,2048]{2,1,0:T(1,128)S(1)}, u32[]{:S(2)}, u32[]{:S(2)}) collective-permute-start(f32[2,1,2048]{2,1,0:T(1,128)S(1)} %get-tuple-element.49), channel_id=1, source_target_pairs={{1,0},{2,1},{3,2},{4,3},{5,4},{6,5},{7,6},{9,8},{10,9},{11,10},{12... | collective-permute-start | bytes 49160 | tf_op jit(solution)/shard_map/ppermute | solution.py:36
  215.0 47.3 %collective-permute-start.8 = (f32[2,1,2048]{2,1,0:T(1,128)S(1)}, f32[2,1,2048]{2,1,0:T(1,128)S(1)}, u32[]{:S(2)}, u32[]{:S(2)}) collective-permute-start(f32[2,1,2048]{2,1,0:T(1,128)S(1)} %get-tuple-element.50), channel_id=1, source_target_pairs={{0,1},{1,2},{2,3},{3,4},{4,5},{5,6},{6,7},{8,9},{9,10},{10,11},{11... | collective-permute-start | bytes 49160 | tf_op jit(solution)/shard_map/ppermute | solution.py:34
  257.0 5.9 %copy-start.7 = (f32[2,8,2047]{2,1,0:T(8,128)S(1)}, f32[2,8,2047]{2,1,0:T(8,128)}, u32[]{:S(2)}) copy-start(f32[2,8,2047]{2,1,0:T(8,128)} %get-tuple-element.47) | copy-start | bytes 393028
  257.0 5.9 %copy-start.8 = (f32[2,8,2047]{2,1,0:T(8,128)S(1)}, f32[2,8,2047]{2,1,0:T(8,128)}, u32[]{:S(2)}) copy-start(f32[2,8,2047]{2,1,0:T(8,128)} %get-tuple-element.48) | copy-start | bytes 393028
  349.8 8.9 %collective-permute-start.13 = (f32[2,1024]{1,0:T(2,128)S(1)}, f32[2,1024]{1,0:T(2,128)S(1)}, u32[]{:S(2)}, u32[]{:S(2)}) collective-permute-start(f32[2,1024]{1,0:T(2,128)S(1)} %bitcast.147), channel_id=1, source_target_pairs={{8,0},{16,8},{24,16},{32,24},{40,32},{48,40},{56,48},{64,56},{72,6... | collective-permute-start | bytes 24584 | tf_op jit(solution)/shard_map/ppermute | solution.py:23
  359.5 10.5 %collective-permute-start.14 = (f32[2,1024]{1,0:T(2,128)S(1)}, f32[2,1024]{1,0:T(2,128)S(1)}, u32[]{:S(2)}, u32[]{:S(2)}) collective-permute-start(f32[2,1024]{1,0:T(2,128)S(1)} %get-tuple-element.34), channel_id=1, source_target_pairs={{0,8},{8,16},{16,24},{24,32},{32,40},{40,48},{48,56},{56,64},{64,7... | collective-permute-start | bytes 24584 | tf_op jit(solution)/shard_map/ppermute | solution.py:23
  364.4 51.9 %collective-permute-start.11 = (f32[2,1,2048]{2,1,0:T(1,128)}, f32[2,1,2048]{2,1,0:T(1,128)S(1)}, u32[]{:S(2)}, u32[]{:S(2)}) collective-permute-start(f32[2,1,2048]{2,1,0:T(1,128)} %get-tuple-element.45), channel_id=1, source_target_pairs={{1,0},{2,1},{3,2},{4,3},{5,4},{6,5},{7,6},{9,8},{10,9},{11,10},{12... | collective-permute-start | bytes 49160 | tf_op jit(solution)/shard_map/ppermute | solution.py:36
  366.9 49.4 %collective-permute-start.12 = (f32[2,1,2048]{2,1,0:T(1,128)}, f32[2,1,2048]{2,1,0:T(1,128)}, u32[]{:S(2)}, u32[]{:S(2)}) collective-permute-start(f32[2,1,2048]{2,1,0:T(1,128)} %get-tuple-element.46), channel_id=1, source_target_pairs={{0,1},{1,2},{2,3},{3,4},{4,5},{5,6},{6,7},{8,9},{9,10},{10,11},{11... | collective-permute-start | bytes 49160 | tf_op jit(solution)/shard_map/ppermute | solution.py:34
  (8 other events, 33.1 us)
